TPU v7x, 256 devices: a whole 4x4x8 slice. The times are simulated.
256 devices in a mesh: dom: 32 (over z, y), rep: 8 (over x, core).
Axes of the slice: x: 4, y: 4, z: 8, core: 2. Of those that a mesh axis runs over, the one named last changes fastest.
Arguments:
- history_in: bfloat16 [256, 128, 1024], P('dom'), may hold values from -6 to 6
- batch_emb: bfloat16 [32768, 1024], P(('dom', 'rep')), may hold values from -6 to 6
- weight: bfloat16 [1024, 1024], P(None, 'rep'), may hold values from -0.1875 to 0.1875
- grad_fresh: bfloat16 [32768, 1024], P(('dom', 'rep')), may hold values from -6 to 6
- edge_weight: int32 [32768, 8320], P(('dom', 'rep')), may hold values from 0 to 3, as said below
- request_block: int32 [256, 32, 2], P(('dom', 'rep')), may hold values from 0 to 7
- request_count: int32 [256, 32], P(('dom', 'rep')), may hold values from 0 to 2, as said below
- batch_block: int32 [32, 8], P('dom'), may hold values from 0 to 7, as said below
Outputs:
- fresh_history: bfloat16 [256, 128, 1024], P('dom')
- weight_grad: float32 [1024, 1024], P('dom', 'rep')
- input_grad: bfloat16 [32768, 1024], P(('dom', 'rep'))
Inputs may be any that keep to these rules, and one draw needn't show every extreme that they name: `request_count`: for every device, at two owners drawn from the seed the count is 2. `batch_block`: each row names every local block 0 to 7 once. `request_block`: entries of unused slots are arbitrary. `edge_weight`: most entries are zero; a row has about 4 nonzero entries in each block of 128 columns.
All inputs are finite; a program needn't handle non-finite values.
Results may differ from a plain program's by a relative error of at most 0.0056.
Values may be sent and summed in bfloat16 or wider, within the bound.
No kernel may reach another device: no remote copies, remote signals or barrier semaphores. Data moves between devices by JAX's collectives and lax.ppermute only.
A program may use at most 128 MiB of HBM per device.

v0:
```python
import math

import jax
import jax.numpy as jnp
from jax import lax
from jax.sharding import PartitionSpec as P


def silu_slope(value):
    sigma = jax.nn.sigmoid(value)
    return sigma * (1.0 + value * (1.0 - sigma))


def shards(
    history_in,
    batch_emb,
    weight,
    grad_fresh,
    edge_weight,
    request_block,
    request_count,
    batch_block,
):
    owners = lax.axis_size("dom")
    replicas = lax.axis_size("rep")
    rows_here = batch_emb.shape[0]
    block = history_in.shape[1]
    width = history_in.shape[2]
    wanted = request_block[0]
    slots_each = wanted.shape[1]
    valid = (jnp.arange(slots_each, dtype=jnp.int32)[None, :] < request_count[0][:, None]).reshape(
        -1
    )
    column_mask = jnp.concatenate(
        [jnp.ones((rows_here,), jnp.float32), jnp.repeat(valid.astype(jnp.float32), block)]
    )
    weights = edge_weight.astype(jnp.float32) * column_mask[None, :]
    degree = 1.0 + jnp.sum(weights, axis=1)
    scale = lax.rsqrt(degree)
    packed = weights.astype(jnp.bfloat16)
    asked = lax.all_to_all(wanted, "dom", split_axis=0, concat_axis=0, tiled=True)
    served = jnp.take(history_in, asked.reshape(-1), axis=0).reshape(
        owners, slots_each, block, width
    )
    halo = lax.all_to_all(served, "dom", split_axis=0, concat_axis=0, tiled=True)
    sources = jnp.concatenate([batch_emb, halo.reshape(-1, width)], axis=0)
    summed = jnp.dot(packed, sources, preferred_element_type=jnp.float32)
    mixed = (scale[:, None] * (batch_emb.astype(jnp.float32) + summed)).astype(jnp.bfloat16)
    full_weight = lax.all_gather(weight, "rep", axis=1, tiled=True)
    pre = jnp.dot(mixed, full_weight, preferred_element_type=jnp.float32)
    fresh = jax.nn.silu(pre).astype(jnp.bfloat16)
    gathered = lax.all_gather(fresh.reshape(-1, block, width), "rep", axis=0, tiled=True)
    fresh_history = jnp.zeros_like(history_in).at[batch_block[0]].set(gathered)
    gated = (grad_fresh.astype(jnp.float32) * silu_slope(pre)).astype(jnp.bfloat16)
    term = lax.dot_general(
        mixed, gated, (((0,), (0,)), ((), ())), preferred_element_type=jnp.float32
    )
    backward = lax.dot_general(
        gated, full_weight, (((1,), (1,)), ((), ())), preferred_element_type=jnp.float32
    )
    back = scale[:, None] * backward
    local = weights[:, :rows_here]
    grad_rows = back + jnp.dot(local.T, back, precision=lax.Precision.HIGHEST)
    input_grad = grad_rows.astype(jnp.bfloat16)
    total_rows = rows_here * owners * replicas
    whole = lax.psum(term, ("dom", "rep"))
    height = width // owners
    across = width // replicas
    share = lax.dynamic_slice(
        whole, (lax.axis_index("dom") * height, lax.axis_index("rep") * across), (height, across)
    )
    weight_grad = share / math.sqrt(total_rows)
    return (fresh_history, weight_grad, input_grad)


def solution(mesh):
    placed = (
        P("dom", None, None),
        P(("dom", "rep"), None),
        P(None, "rep"),
        P(("dom", "rep"), None),
        P(("dom", "rep"), None),
        P(("dom", "rep"), None, None),
        P(("dom", "rep"), None),
        P("dom", None),
    )
    return jax.shard_map(
        shards,
        mesh=mesh,
        in_specs=placed,
        out_specs=(P("dom", None, None), P("dom", "rep"), P(("dom", "rep"), None)),
        check_vma=False,
    )
```

profile of v0, /device:TPU:1, one launch (start us, length us, event | category | flops | bytes accessed | tf_op | source)
XLA Modules:
  0.0 777.9 jit_solution(7063605258533965794)
XLA Ops:
  7.2 0.9 copy.15
  8.1 20.4 %all_to_all.14 = s32[32,1,2]{2,1,0:T(1,128)S(1)} all-to-all(s32[32,1,2]{2,1,0:T(1,128)S(1)} %copy.15), channel_id=1, replica_groups=mesh['dom'=32,'rep'=8] {'dom'}, dimensions={0} | all-to-all | bytes 512 | tf_op jit(solution)/shard_map/all_to_all | solution.py:41
  28.5 0.5 broadcast.79
  29.0 0.7 reduce.3
  29.7 0.1 reshape.105
  29.8 0.1 copy.16
  29.9 0.1 copy.17
  30.0 7.5 gather_fusion
  37.6 14.2 %broadcast_select_fusion = bf16[32,2,128,1024]{3,2,1,0:T(8,128)(2,1)} fusion(bf16[32,2,128,1024]{3,2,1,0:T(8,128)(2,1)} %bitcast.20, pred[32,2]{1,0:T(8,128)(4,1)S(1)} %copy.17), kind=kLoop, calls=%fused_computation.6 | loop fusion | flops 8388608 | bytes 33554496 | tf_op jit(solution)/shard_map/jit(_take)/select_n | solution.py:42
  51.8 5.3 all-to-all-start.1
  57.1 0.0 all-gather.4.cloned.1.call-start
  57.2 0.7 all-gather.4.cloned.1.call-update
  57.9 0.0 all-reduce.3.cloned.1.call-start
  57.9 0.1 fusion.22
  58.0 0.1 reshape.108
  58.1 0.1 broadcast_bitcast_fusion
  58.2 4.7 fusion.27
  63.0 365.8 %all-to-all-done.1 = bf16[32,2,128,1024]{3,2,1,0:T(8,128)(2,1)} async-done(((bf16[32,2,128,1024]{3,2,1,0:T(8,128)(2,1)}), bf16[32,2,128,1024]{3,2,1,0:T(8,128)(2,1)}, u32[]{:S(2)}, u32[]{:S(2)}) %all-to-all-start.1) | async-done | bytes 16777248 | tf_op jit(solution)/shard_map/all_to_all | solution.py:45
  428.8 8.3 %fusion.16 = bf16[128,1024]{1,0:T(8,128)(2,1)S(1)} fusion(bf16[8192,1024]{1,0:T(8,128)(2,1)} %bitcast.8, bf16[128,1024]{1,0:T(8,128)(2,1)S(1)} %copy-done.4, f32[128,8320]{1,0:T(8,128)} %get-tuple-element.4, f32[128]{0:T(128)S(1)} %add_rsqrt_fusion), kind=kOutput, calls=%fused_computation.14 | convolution fusion | flops 2216706048 | bytes 21561856 | tf_op jit(solution)/shard_map/dot_general | solution.py:47
  437.1 0.0 all-gather.4.cloned.1.call-done
  437.1 2.8 multiply_convert_fusion.1
  439.9 2.8 fusion.26
  442.7 0.0 all-reduce.3.cloned.1.call-update
  442.8 0.0 all-gather.6.cloned.1.call-start
  442.8 0.7 all-gather.6.cloned.1.call-update
  443.5 2.4 convolution_multiply_fusion
  446.0 2.3 fusion.15
  448.3 284.7 %all-reduce.3.cloned.1.call-done = f32[1024,1024]{1,0:T(8,128)} async-done(((f32[1024,1024]{1,0:T(8,128)}), f32[1024,1024]{1,0:T(8,128)}) %all-reduce.3.cloned.1.call-update) | async-done | bytes 4194320 | tf_op jit(solution)/shard_map/psum | solution.py:66
  733.0 1.3 dynamic-slice_multiply_fusion
  734.3 29.7 %all-gather.6.cloned.1.call-done = bf16[1024,1024]{1,0:T(8,128)(2,1)} async-done(((bf16[128,1024]{1,0:T(8,128)(2,1)}), bf16[1024,1024]{1,0:T(8,128)(2,1)}) %all-gather.6.cloned.1.call-update) | async-done | bytes 2097168 | tf_op jit(solution)/shard_map/all_gather | solution.py:52
  764.0 1.6 broadcast_in_dim.21
  765.6 5.7 scatter_fusion
  (18 shorter events, 0.1 us)
Async XLA Ops:
  7.2 22.9 %copy-start = (bf16[8,128,1024]{2,1,0:T(8,128)(2,1)S(1)}, bf16[8,128,1024]{2,1,0:T(8,128)(2,1)}, u32[]{:S(2)}) copy-start(bf16[8,128,1024]{2,1,0:T(8,128)(2,1)} %param.8) | copy-start | bytes 6291460
  51.8 6.1 copy-start.3
  51.8 377.0 %all-to-all-start.1 = ((bf16[32,2,128,1024]{3,2,1,0:T(8,128)(2,1)}), bf16[32,2,128,1024]{3,2,1,0:T(8,128)(2,1)}, u32[]{:S(2)}, u32[]{:S(2)}) async-start(bf16[32,2,128,1024]{3,2,1,0:T(8,128)(2,1)} %broadcast_select_fusion), calls=%async_computation.1 | async-start | bytes 33554432 | tf_op jit(solution)/shard_map/all_to_all | solution.py:45
  57.1 380.0 %all-gather.4.cloned.1.call-start = ((), (), s32[]{:S(2)}) async-start(), calls=%async_computation.2 | async-start | bytes 2359296 | tf_op jit(solution)/shard_map/all_gather | solution.py:49
  57.9 675.1 %all-reduce.3.cloned.1.call-start = ((), (), s32[]{:S(2)}) async-start(), calls=%async_computation.3 | async-start | bytes 8388608 | tf_op jit(solution)/shard_map/psum | solution.py:66
  58.2 370.6 %copy-start.4 = (bf16[128,1024]{1,0:T(8,128)(2,1)S(1)}, bf16[128,1024]{1,0:T(8,128)(2,1)}, u32[]{:S(2)}) copy-start(bf16[128,1024]{1,0:T(8,128)(2,1)} %param.9) | copy-start | bytes 786436
  437.1 2.9 copy-start.2
  439.9 3.6 copy-start.5
  442.8 321.3 %all-gather.6.cloned.1.call-start = ((), (), s32[]{:S(2)}) async-start(), calls=%async_computation.4 | async-start | bytes 2359296 | tf_op jit(solution)/shard_map/all_gather | solution.py:52
  446.0 325.4 %copy-start.1 = (bf16[8,128,1024]{2,1,0:T(8,128)(2,1)S(1)}, bf16[8,128,1024]{2,1,0:T(8,128)(2,1)}, u32[]{:S(2)}) copy-start(bf16[8,128,1024]{2,1,0:T(8,128)(2,1)} %param.8) | copy-start | bytes 6291460
Sparse Core Ops, SparseCore 0:
  59.8 32.8 all-gather.3
  442.9 290.0 all-reduce.2
  735.6 28.3 all-gather.5
where the time goes:
time: 778 us
  waiting for transfers between devices  682 us (88%)
  other arithmetic  21.1 us (3%)
  blocking collectives  20.4 us (3%)
  matrix products  18.7 us (2%)
  local copies, waits for them, and re-layouts  16.7 us (2%)
  between operations  13.9 us (2%)
    all_to_all x1, waiting for transfers between devices, shards(): lax.all_to_all(served, 'dom', split_axis=0, concat_axis=0, tiled=True)  366 us
    psum x1, waiting for transfers between devices, shards(): whole = lax.psum(term, ('dom', 'rep'))  285 us
    all_gather x1, waiting for transfers between devices, shards(): lax.all_gather(fresh.reshape(-1, block, width), 'rep', axis=0, tiled=True)  29.7 us
    all_to_all x1, blocking collectives, shards(): lax.all_to_all(wanted, 'dom', split_axis=0, concat_axis=0, tiled=True)  20.4 us
  transfers between devices with their start and end apart: 4, of which 3 were waited for; matrix products, arithmetic and copies ran while one was open for 2% of the time, Pallas kernels for 0%

commit v1 on v0

v1 whole, which is shorter than its diff:
```python
import functools
import math

import jax
import jax.numpy as jnp
from jax import lax
from jax.experimental import pallas as pl
from jax.experimental.pallas import tpu as pltpu
from jax.sharding import PartitionSpec as P

Z, Y, X, CORES = 8, 4, 4, 2
CAP = 2
BLOCK = 128
NAMES = 16
BF16 = jnp.bfloat16
F32 = jnp.float32
VMEM = pl.BlockSpec(memory_space=pltpu.VMEM)
SMEM = pl.BlockSpec(memory_space=pltpu.SMEM)
LIMIT = 50 * 2**20


def shift_z(value, step):
    pairs = [(z * Y + y, (z + step) % Z * Y + y) for z in range(Z) for y in range(Y)]
    return lax.ppermute(value, "dom", pairs)


def shift_y(value, step):
    pairs = [(z * Y + y, z * Y + (y + step) % Y) for z in range(Z) for y in range(Y)]
    return lax.ppermute(value, "dom", pairs)


def shift_x(value, step):
    pairs = [(x * CORES + c, (x + step) % X * CORES + c) for x in range(X) for c in range(CORES)]
    return lax.ppermute(value, "rep", pairs)


def swap_core(value):
    pairs = [(x * CORES + c, x * CORES + 1 - c) for x in range(X) for c in range(CORES)]
    return lax.ppermute(value, "rep", pairs)


def slope(value):
    sigma = 1.0 / (1.0 + jnp.exp(-value))
    return sigma * (1.0 + value * (1.0 - sigma))


def params():
    return pltpu.CompilerParams(vmem_limit_bytes=LIMIT)


def cost(flops, moved):
    return pl.CostEstimate(flops=flops, bytes_accessed=moved, transcendentals=0)


def pack_kernel(at_ref, edge_ref, code_ref, batch_ref, *outs):
    near, (keep_ref, give_ref, local_ref, scale_ref) = outs[:Y], outs[Y:]
    y, core = at_ref[0], at_ref[1]
    rows, width = batch_ref.shape
    half = width // CORES
    pair = CAP * BLOCK
    sums = jnp.zeros((rows, pair), jnp.int32)
    for step in range(Y):
        column = lax.rem(y + step, Y)
        for z in range(Z):
            slot = z * Y + column
            edges = edge_ref[:, pl.ds(pl.multiple_of(rows + slot * pair, BLOCK), pair)]
            code = code_ref[pl.ds(slot, 1), :]
            near[step][z, :rows, :] = edges.astype(F32).astype(BF16)
            near[step][z, rows:, :] = jnp.broadcast_to(code, (NAMES, pair)).astype(F32).astype(BF16)
            sums = sums + jnp.where(code >= 0, edges, 0)
    local = edge_ref[:, :rows].astype(F32)
    degree = (
        1.0
        + jnp.sum(local, axis=1, keepdims=True)
        + jnp.sum(sums.astype(F32), axis=1, keepdims=True)
    )
    scale = jnp.broadcast_to(lax.rsqrt(degree), (rows, BLOCK))
    scale_ref[...] = scale
    local_ref[...] = local.astype(BF16)
    for ref, part in ((keep_ref, core), (give_ref, 1 - core)):
        batch = batch_ref[:, pl.ds(pl.multiple_of(part * half, BLOCK), half)]
        ref[:, :half] = batch.astype(F32) + jnp.dot(
            local.astype(BF16), batch, preferred_element_type=F32
        )
        ref[:, half:] = scale


def pack(at, edge_weight, code, batch_emb):
    rows, width = batch_emb.shape
    half = width // CORES
    message = jax.ShapeDtypeStruct((Z, rows + NAMES, CAP * BLOCK), BF16)
    own = jax.ShapeDtypeStruct((rows, half + BLOCK), F32)
    return pl.pallas_call(
        pack_kernel,
        out_shape=[message] * Y
        + [
            own,
            own,
            jax.ShapeDtypeStruct((rows, rows), BF16),
            jax.ShapeDtypeStruct((rows, BLOCK), F32),
        ],
        in_specs=[SMEM, VMEM, VMEM, VMEM],
        out_specs=[VMEM] * (Y + 4),
        compiler_params=params(),
        cost_estimate=cost(2 * rows * rows * width, 8 * 2**20),
        name="pack",
    )(at, edge_weight, code, batch_emb)


def split_kernel(first_ref, second_ref, low_ref, high_ref):
    low_ref[...] = first_ref[...]
    high_ref[...] = second_ref[...]


def split(first, second, rows):
    tile = BLOCK
    steps = rows // tile
    part = jax.ShapeDtypeStruct((rows, first.shape[1]), first.dtype)
    spec = pl.BlockSpec((tile, first.shape[1]), lambda i: (i, 0))
    return pl.pallas_call(
        split_kernel,
        grid=(steps,),
        out_shape=[part, part],
        in_specs=[spec, pl.BlockSpec((tile, first.shape[1]), lambda i: (i + steps, 0))],
        out_specs=[spec, spec],
        compiler_params=params(),
        cost_estimate=cost(0, 4 * rows * first.shape[1] * 2),
        name="split",
    )(first, second)


def serve_kernel(owners, pieces, first, last, at_ref, *refs):
    senders = CORES * Y
    count = owners * senders
    messages, refs = refs[:count], refs[count:]
    tables, refs = refs[: sum(pieces)], refs[sum(pieces) :]
    if not first:
        total_ref, refs = refs[0], refs[1:]
    outs, merged = refs[:-1], refs[-1]
    depth = merged.shape[1] // owners
    blocks = depth // BLOCK

    @pl.when(pl.program_id(0) == 0)
    def _():
        for owner in range(owners):
            for sender in range(senders):
                ref = messages[owner * senders + sender]
                names = ref[0, BLOCK:, :].astype(F32)
                body = ref[0, :BLOCK, :].reshape(BLOCK // NAMES, NAMES, CAP * BLOCK)
                for block in range(blocks):
                    hit = jnp.where(names == float(block), 1.0, 0.0).astype(BF16)
                    part = body * hit[None]
                    both = part[:, :, :BLOCK] + part[:, :, BLOCK:]
                    merged[
                        sender * BLOCK : (sender + 1) * BLOCK,
                        owner * depth + block * BLOCK : owner * depth + (block + 1) * BLOCK,
                    ] = both.reshape(BLOCK, BLOCK)

    for step in range(Y):
        products = []
        for core in range(CORES):
            sender = core * Y + step
            rows = slice(sender * BLOCK, (sender + 1) * BLOCK)
            value = None if first else total_ref[core, step]
            start = 0
            for table in tables:
                product = jnp.dot(
                    merged[rows, start : start + table.shape[0]],
                    table[...],
                    preferred_element_type=F32,
                )
                value = product if value is None else value + product
                start += table.shape[0]
            products.append(value)
        for core in range(CORES):
            if last:
                outs[step][core] = products[core].astype(outs[step].dtype)
            else:
                outs[0][core, step] = products[core]


def serve(at, messages, tables, total=None, last=False, chunk=256):
    owners = len(tables)
    depth = sum(piece.shape[0] for piece in tables[0])
    half = tables[0][0].shape[1]
    flat = [piece for pieces in tables for piece in pieces]
    rows = messages[0].shape[1]

    def message_spec(owner):
        return pl.BlockSpec((1, rows, CAP * BLOCK), lambda j, at_ref: (at_ref[owner], 0, 0))

    in_specs = [message_spec(owner) for owner in range(owners) for _ in messages]
    in_specs += [pl.BlockSpec((piece.shape[0], chunk), lambda j, at_ref: (0, j)) for piece in flat]
    total_spec = pl.BlockSpec((CORES, Y, BLOCK, chunk), lambda j, at_ref: (0, 0, 0, j))
    args = list(messages) * owners + flat
    if total is not None:
        in_specs.append(total_spec)
        args.append(total)
    if last:
        out_shape = [
            jax.ShapeDtypeStruct((CORES, BLOCK, half), F32 if step == 0 else BF16)
            for step in range(Y)
        ]
        out_specs = [
            pl.BlockSpec((CORES, BLOCK, chunk), lambda j, at_ref: (0, 0, j)) for _ in range(Y)
        ]
    else:
        out_shape = [jax.ShapeDtypeStruct((CORES, Y, BLOCK, half), F32)]
        out_specs = [total_spec]
    kernel = functools.partial(
        serve_kernel, owners, [len(pieces) for pieces in tables], total is None, last
    )
    senders = CORES * Y * BLOCK
    result = pl.pallas_call(
        kernel,
        grid_spec=pltpu.PrefetchScalarGridSpec(
            num_scalar_prefetch=1,
            grid=(half // chunk,),
            in_specs=in_specs,
            out_specs=out_specs,
            scratch_shapes=[pltpu.VMEM((senders, owners * depth), BF16)],
        ),
        out_shape=out_shape,
        compiler_params=params(),
        cost_estimate=cost(2 * senders * owners * depth * half, owners * 2 * 2**20),
        name="serve",
    )(at, *args)
    return result if last else result[0]


def mix_kernel(keep_ref, peer_ref, own_ref, *refs):
    arrived, out_ref = refs[:-1], refs[-1]
    half = own_ref.shape[2]
    for core, ref in enumerate((keep_ref, peer_ref)):
        value = ref[:, :half] + own_ref[core]
        for part in arrived:
            value = value + part[core].astype(F32)
        scale = ref[:, half : half + 1]
        out_ref[core] = (scale * value).astype(BF16)


def mix(keep, peer, own, arrived):
    return pl.pallas_call(
        mix_kernel,
        out_shape=jax.ShapeDtypeStruct(own.shape, BF16),
        in_specs=[VMEM] * (3 + len(arrived)),
        out_specs=VMEM,
        compiler_params=params(),
        cost_estimate=cost(2**20, 2 * 2**20),
        name="mix",
    )(keep, peer, own, *arrived)


def halves(at_ref, ref):
    core = at_ref[1]
    half = ref.shape[0] // CORES
    mine = ref[pl.ds(pl.multiple_of(core * half, BLOCK), half), :]
    other = ref[pl.ds(pl.multiple_of((1 - core) * half, BLOCK), half), :]
    return mine, other


def row_pair(mine_ref, other_ref):
    shape = (CORES * BLOCK, mine_ref.shape[2])
    mine = mine_ref[...].reshape(shape)
    other = jnp.concatenate([other_ref[1], other_ref[0]], axis=0)
    return mine, other


def term_kernel(at_ref, weight_ref, grads_ref, *refs):
    mixed, outs, whole_ref = refs[: 2 * X], refs[2 * X : -1], refs[-1]
    core = at_ref[1]
    weight_mine, weight_other = halves(at_ref, weight_ref)
    half = weight_mine.shape[0]
    sums = [None, None]
    for step in range(X):
        rows = row_pair(mixed[2 * step], mixed[2 * step + 1])
        pre = jnp.dot(rows[0], weight_mine, preferred_element_type=F32) + jnp.dot(
            rows[1], weight_other, preferred_element_type=F32
        )
        grads = jnp.concatenate(
            [grads_ref[at_ref[2 + 2 * step + part]] for part in range(CORES)], axis=0
        )
        gated = (grads.astype(F32) * slope(pre)).T.astype(BF16)
        for part in range(CORES):
            product = jnp.dot(gated, rows[part], preferred_element_type=F32)
            sums[part] = product if sums[part] is None else sums[part] + product
    height = half // (Z * Y // CORES)
    whole_ref[pl.ds(pl.multiple_of(core * half, BLOCK), half), :] = sums[0].T
    whole_ref[pl.ds(pl.multiple_of((1 - core) * half, BLOCK), half), :] = sums[1].T
    for step, out_ref in enumerate(outs):
        column = lax.rem(at_ref[0] - step + Y, Y)
        for z in range(Z):
            start = pl.multiple_of((z * Y + column) * height, height)
            out_ref[z * height : (z + 1) * height, :] = whole_ref[pl.ds(start, height), :]


def weight_term(at, weight, grads, mixed):
    return pl.pallas_call(
        term_kernel,
        out_shape=[jax.ShapeDtypeStruct((weight.shape[0] // Y, weight.shape[1]), F32)] * Y,
        in_specs=[SMEM] + [VMEM] * (2 + len(mixed)),
        out_specs=[VMEM] * Y,
        scratch_shapes=[pltpu.VMEM(weight.shape, F32)],
        compiler_params=params(),
        cost_estimate=cost(2**29, 3 * 2**20),
        name="term",
    )(at, weight, grads, *mixed)


def fresh_kernel(at_ref, weight_ref, *refs):
    mixed, out_ref = refs[:-1], refs[-1]
    weight_mine, weight_other = halves(at_ref, weight_ref)
    for step in range(X):
        rows = row_pair(mixed[2 * step], mixed[2 * step + 1])
        pre = jnp.dot(rows[0], weight_mine, preferred_element_type=F32) + jnp.dot(
            rows[1], weight_other, preferred_element_type=F32
        )
        value = (pre / (1.0 + jnp.exp(-pre))).astype(BF16)
        for part in range(CORES):
            place = at_ref[2 + X * CORES + 2 * step + part]
            out_ref[place] = value[part * BLOCK : (part + 1) * BLOCK]


def fresh_blocks(at, weight, mixed):
    width = weight.shape[0]
    return pl.pallas_call(
        fresh_kernel,
        out_shape=jax.ShapeDtypeStruct((X * CORES, BLOCK, width), BF16),
        in_specs=[SMEM] + [VMEM] * (1 + len(mixed)),
        out_specs=VMEM,
        compiler_params=params(),
        cost_estimate=cost(2**31, 6 * 2**20),
        name="fresh",
    )(at, weight, *mixed)


def back_kernel(at_ref, weight_ref, mine_ref, other_ref, grad_ref, scale_ref, local_ref, out_ref):
    weight_mine, weight_other = halves(at_ref, weight_ref)
    pre = jnp.dot(mine_ref[0], weight_mine, preferred_element_type=F32) + jnp.dot(
        other_ref[1], weight_other, preferred_element_type=F32
    )
    gated = (grad_ref[...].astype(F32) * slope(pre)).astype(BF16)
    back = scale_ref[:, :1] * lax.dot_general(
        gated, weight_ref[...], (((1,), (1,)), ((), ())), preferred_element_type=F32
    )
    local = local_ref[...].astype(F32).T.astype(BF16)
    value, rest = back, back
    for _ in range(3):
        part = rest.astype(BF16)
        value = value + jnp.dot(local, part, preferred_element_type=F32)
        rest = rest - part.astype(F32)
    out_ref[...] = value.astype(BF16)


def input_rows(at, weight, mine, other, grad_fresh, scale, local):
    return pl.pallas_call(
        back_kernel,
        out_shape=jax.ShapeDtypeStruct(grad_fresh.shape, BF16),
        in_specs=[SMEM] + [VMEM] * 6,
        out_specs=VMEM,
        compiler_params=params(),
        cost_estimate=cost(2**29 + 2**28, 4 * 2**20),
        name="back",
    )(at, weight, mine, other, grad_fresh, scale, local)


def shards(
    history_in,
    batch_emb,
    weight,
    grad_fresh,
    edge_weight,
    request_block,
    request_count,
    batch_block,
):
    owner = lax.axis_index("dom")
    replica = lax.axis_index("rep")
    z, y = owner // Y, owner % Y
    x, core = replica // CORES, replica % CORES
    blocks, block, width = history_in.shape
    rows = batch_emb.shape[0]
    half = width // CORES

    table = lax.dynamic_slice(history_in, (0, 0, core * half), (blocks, block, half))
    table = table.reshape(blocks * block, half)
    up, down = [table, shift_z(table, 1)], [table, shift_z(table, -1)]

    offsets = jnp.array([0, X - 1, 1, 2], jnp.int32)
    places = ((x + offsets) % X)[:, None] * CORES + jnp.stack([core, 1 - core])[None, :]
    places = places.reshape(-1)
    targets = jnp.take(batch_block[0], places)
    at = jnp.concatenate([jnp.stack([y, core]), places, targets]).astype(jnp.int32)

    valid = jnp.arange(CAP, dtype=jnp.int32)[None, :] < request_count[0][:, None]
    code = jnp.where(valid, request_block[0], -1)
    code = jnp.repeat(code, block, axis=1)
    *near, keep, give, local, scale = pack(at, edge_weight, code, batch_emb)
    peer = swap_core(give)
    here = [near[0]] + [shift_y(near[step], step) for step in range(1, Y)]

    full_weight = lax.all_gather(weight, "rep", axis=1, tiled=True)
    grads = lax.all_to_all(grad_fresh, "rep", split_axis=1, concat_axis=0, tiled=True)
    grads = grads.reshape(X * CORES, rows, -1)

    def owners_at(*steps):
        return jnp.stack([(z + step) % Z for step in steps]).astype(jnp.int32)

    up[1], down[1], here[1], here[3] = lax.optimization_barrier(
        (up[1], down[1], here[1], here[3])
    )
    up.append(shift_z(up[1], 1))
    down.append(shift_z(down[1], -1))
    up[2], down[2], here[2], grads, peer = lax.optimization_barrier(
        (up[2], down[2], here[2], grads, peer)
    )
    up.append(shift_z(up[2], 1))
    down.append(shift_z(down[2], -1))
    messages = here + [swap_core(message) for message in here]
    total = serve(owners_at(0, 7, 1), messages, [[table], [up[1]], [down[1]]])
    total = serve(owners_at(6, 2), messages, [[up[2]], [down[2]]], total)
    up[3], down[3], total = lax.optimization_barrier((up[3], down[3], total))
    middle = blocks * block // 2
    low, high = split(up[3], down[3], middle)
    far = [shift_z(low, 1), shift_z(high, -1)]
    total = serve(owners_at(5, 3), messages, [[up[3]], [down[3]]], total)
    sums = serve(owners_at(4), messages, [far], total, last=True)

    arrived = [shift_y(sums[step], -step) for step in range(1, Y)]
    mixed = [mix(keep, peer, sums[0], arrived)]
    mixed += [shift_x(mixed[0], 1), shift_x(mixed[0], -1), shift_x(mixed[0], 2)]
    own_other = swap_core(mixed[0])
    input_grad = input_rows(at, full_weight, mixed[0], own_other, grad_fresh, scale, local)
    mixed[3], input_grad = lax.optimization_barrier((mixed[3], input_grad))
    mixed = [mixed[0], own_other] + [
        part for mine in mixed[1:] for part in (mine, swap_core(mine))
    ]
    columns = [[z * Y + column for z in range(Z)] for column in range(Y)]
    terms = weight_term(at, weight, grads, mixed)
    others = [shift_y(terms[step], -step) for step in range(1, Y)]
    fresh_history = fresh_blocks(at, full_weight, mixed)
    others, fresh_history = lax.optimization_barrier((others, fresh_history))
    part = terms[0] + others[0] + others[1] + others[2]
    part = lax.all_to_all(
        part, "dom", split_axis=0, concat_axis=0, tiled=True, axis_index_groups=columns
    )
    total_rows = rows * Z * Y * X * CORES
    weight_grad = jnp.sum(part.reshape(Z, -1, weight.shape[1]), axis=0) / math.sqrt(total_rows)
    return (fresh_history, weight_grad, input_grad)


def solution(mesh):
    placed = (
        P("dom", None, None),
        P(("dom", "rep"), None),
        P(None, "rep"),
        P(("dom", "rep"), None),
        P(("dom", "rep"), None),
        P(("dom", "rep"), None, None),
        P(("dom", "rep"), None),
        P("dom", None),
    )
    return jax.shard_map(
        shards,
        mesh=mesh,
        in_specs=placed,
        out_specs=(P("dom", None, None), P("dom", "rep"), P(("dom", "rep"), None)),
        check_vma=False,
    )
```

time: 778 us -> 188 us (0.24)
  waiting for transfers between devices: 682 us -> 53.3 us
  Pallas kernels: 0 us -> 47.8 us
  starting transfers between devices: 5.44 us -> 46.2 us
  other arithmetic: 21.1 us -> 1.13 us
  matrix products: 18.7 us -> 0 us
  blocking collectives: 20.4 us -> 12.2 us
    all_to_all x1, waiting for transfers between devices: 366 us -> 1.79 us  [shards(): lax.all_to_all(grad_fresh, 'rep', split_axis=1, concat_axis=0, tiled=True)]
    psum x1 -> x0, waiting for transfers between devices: 285 us -> none  [shards(): whole = lax.psum(term, ('dom', 'rep'))]
    ppermute x0 -> x29, waiting for transfers between devices: none -> 51.5 us  [the longest x9 31.6 us: shift_y(): return lax.ppermute(value, 'dom', pairs)]
    pallas_call x0 -> x10, Pallas kernels: none -> 47.8 us  [the longest x4 27.9 us: serve(): pl.pallas_call(kernel, grid_spec=pltpu.PrefetchScalarGridSpec(num_scalar_...]
    ppermute x0 -> x29, starting transfers between devices: none -> 41.4 us  [the longest x8 14.5 us: shift_z(): return lax.ppermute(value, 'dom', pairs)]
    all_gather x1 -> x0, waiting for transfers between devices: 29.7 us -> none  [shards(): lax.all_gather(fresh.reshape(-1, block, width), 'rep', axis=0, tiled=True)]
    dot_general x5 -> x0, matrix products: 18.7 us -> none  [the longest x1 8.29 us: shards(): summed = jnp.dot(packed, sources, preferred_element_type=jnp.float32)]
    select_n x3, other arithmetic: 14.3 us -> 0.01 us  [the longest x2 0.01 us: shards(): targets = jnp.take(batch_block[0], places)]
  transfers between devices with their start and end apart: 4 -> 31, of which waited for: 3 -> 14; matrix products, arithmetic and copies ran while one was open for 2% -> 2% of each run, Pallas kernels for 0% -> 24%
where the time goes in v1:
time: 188 us; the launch traced here: 186 us
  waiting for transfers between devices  53.3 us (28%)
  Pallas kernels  47.8 us (25%)
  starting transfers between devices  46.2 us (25%)
  between operations  14.3 us (8%)
  blocking collectives  12.2 us (6%)
  local copies, waits for them, and re-layouts  11.3 us (6%)
    ppermute x9, waiting for transfers between devices, shift_y(): return lax.ppermute(value, 'dom', pairs)  31.6 us
    pallas_call x4, Pallas kernels, serve(): pl.pallas_call(kernel, grid_spec=pltpu.PrefetchScalarGridSpec(num_scalar_...  27.9 us
    ppermute x8, starting transfers between devices, shift_z(): return lax.ppermute(value, 'dom', pairs)  14.5 us
    ppermute x8, waiting for transfers between devices, shift_z(): return lax.ppermute(value, 'dom', pairs)  13.5 us
    all_to_all x1, blocking collectives, shards(): lax.all_to_all(part, 'dom', split_axis=0, concat_axis=0, tiled=True, axis...  12.2 us
    ppermute x9, starting transfers between devices, swap_core(): return lax.ppermute(value, 'rep', pairs)  11.4 us
    ppermute x9, starting transfers between devices, shift_y(): return lax.ppermute(value, 'dom', pairs)  10.1 us
    unnamed x36, local copies, waits for them, and re-layouts  7.49 us
  transfers between devices with their start and end apart: 31, of which 14 were waited for; matrix products, arithmetic and copies ran while one was open for 2% of the time, Pallas kernels for 24%

profile of v1, /device:TPU:1, one launch (start us, length us, event | category | flops | bytes accessed | tf_op | source)
XLA Modules:
  0.0 186.3 jit_solution(11631857683982580794)
XLA Ops:
  9.8 2.5 %collective-permute-start = (bf16[1024,512]{1,0:T(8,128)(2,1)}, bf16[1024,512]{1,0:T(8,128)(2,1)}, u32[]{:S(2)}, u32[]{:S(2)}) collective-permute-start(bf16[1024,512]{1,0:T(8,128)(2,1)} %bitcast.5.refs_24_), channel_id=1, source_target_pairs={{0,32},{8,40},{16,48},{24,56},{32,64},{40,72},{48,80},{56,88},{64,... | collective-permute-start | bytes 3145736 | tf_op jit(solution)/shard_map/ppermute | solution.py:24
  12.3 3.9 %collective-permute-start.1 = (bf16[1024,512]{1,0:T(8,128)(2,1)}, bf16[1024,512]{1,0:T(8,128)(2,1)}, u32[]{:S(2)}, u32[]{:S(2)}) collective-permute-start(bf16[1024,512]{1,0:T(8,128)(2,1)} %bitcast.5.refs_24_), channel_id=1, source_target_pairs={{0,224},{8,232},{16,240},{24,248},{32,0},{40,8},{48,16},{56,24},{6... | collective-permute-start | bytes 3145736 | tf_op jit(solution)/shard_map/ppermute | solution.py:24
  17.6 4.0 %pack.1 = (bf16[8,144,256]{2,1,0:T(8,128)(2,1)S(1)}, bf16[8,144,256]{2,1,0:T(8,128)(2,1)}, bf16[8,144,256]{2,1,0:T(8,128)(2,1)S(1)}, bf16[8,144,256]{2,1,0:T(8,1...) custom-call(s32[18]{0:T(128)S(1)} %pad_add_fusion.1.at_ref, ...), custom_call_target="tpu_custom_call" | custom-call | flops 33554432 | bytes 8388608 | tf_op jit(solution)/shard_map/pack/pallas_call | solution.py:93
  27.9 12.7 %collective-permute-done.2.refs_1_.refs_9_.refs_17_ = bf16[8,144,256]{2,1,0:T(8,128)(2,1)S(1)} collective-permute-done((bf16[8,144,256]{2,1,0:T(8,128)(2,1)}, bf16[8,144,256]{2,1,0:T(8,128)(2,1)S(1)}, u32[]{:S(2)}, u32[]{:S(2)}) %collective-permute-start.2) | collective-permute-done | bytes 589856 | tf_op jit(solution)/shard_map/ppermute | solution.py:29
  40.7 2.7 %collective-permute-start.5 = (bf16[1024,512]{1,0:T(8,128)(2,1)}, bf16[1024,512]{1,0:T(8,128)(2,1)}, u32[]{:S(2)}, u32[]{:S(2)}) collective-permute-start(bf16[1024,512]{1,0:T(8,128)(2,1)} %collective-permute-done.1.refs_26_), channel_id=1, source_target_pairs={{0,224},{8,232},{16,240},{24,248},{32,0},{40,8},{48,16},{56,24},{6... | collective-permute-start | bytes 3145736 | tf_op jit(solution)/shard_map/ppermute | solution.py:24
  43.3 2.3 %collective-permute-start.6 = (bf16[8,144,256]{2,1,0:T(8,128)(2,1)}, bf16[8,144,256]{2,1,0:T(8,128)(2,1)}, u32[]{:S(2)}, u32[]{:S(2)}) collective-permute-start(bf16[8,144,256]{2,1,0:T(8,128)(2,1)} %copy-done.11), channel_id=1, source_target_pairs={{0,16},{8,24},{16,0},{24,8},{32,48},{40,56},{48,32},{56,40},{64,80... | collective-permute-start | bytes 1769480 | tf_op jit(solution)/shard_map/ppermute | solution.py:29
  45.6 3.0 %collective-permute-start.8 = (bf16[8,144,256]{2,1,0:T(8,128)(2,1)S(1)}, bf16[8,144,256]{2,1,0:T(8,128)(2,1)}, u32[]{:S(2)}, u32[]{:S(2)}) collective-permute-start(bf16[8,144,256]{2,1,0:T(8,128)(2,1)S(1)} %get-tuple-element.48.refs_0_.refs_8_.refs_16_), channel_id=1, source_target_pairs={{0,1},{1,0},{2,3},{3,2},{4,5},{5,4},{6,7},{7,6},{8,9},{9,8},{10,11... | collective-permute-start | bytes 1769480 | tf_op jit(solution)/shard_map/ppermute | solution.py:39
  51.3 4.8 %all-to-all-start = ((bf16[128,8,128]{2,0,1:T(8,128)(2,1)}), bf16[128,8,128]{2,0,1:T(8,128)(2,1)}, u32[]{:S(2)}, u32[]{:S(2)}) async-start(bf16[128,8,128]{2,0,1:T(8,128)(2,1)} %copy.15), calls=%async_computation | async-start | bytes 524288 | tf_op jit(solution)/shard_map/all_to_all | solution.py:403
  57.6 3.3 %collective-permute-start.9 = (bf16[8,144,256]{2,1,0:T(8,128)(2,1)S(1)}, bf16[8,144,256]{2,1,0:T(8,128)(2,1)}, u32[]{:S(2)}, u32[]{:S(2)}) collective-permute-start(bf16[8,144,256]{2,1,0:T(8,128)(2,1)S(1)} %collective-permute-done.2.refs_1_.refs_9_.refs_17_), channel_id=1, source_target_pairs={{0,1},{1,0},{2,3},{3,2},{4,5},{5,4},{6,7},{7,6},{8,9},{9,8},{10,11... | collective-permute-start | bytes 1769480 | tf_op jit(solution)/shard_map/ppermute | solution.py:39
  62.7 2.3 %collective-permute-done.4.refs_16_ = bf16[1024,512]{1,0:T(8,128)(2,1)} collective-permute-done((bf16[1024,512]{1,0:T(8,128)(2,1)}, bf16[1024,512]{1,0:T(8,128)(2,1)}, u32[]{:S(2)}, u32[]{:S(2)}) %collective-permute-start.4) | collective-permute-done | bytes 1048608 | tf_op jit(solution)/shard_map/ppermute | solution.py:24
  65.0 2.8 %collective-permute-start.10 = (bf16[8,144,256]{2,1,0:T(8,128)(2,1)}, bf16[8,144,256]{2,1,0:T(8,128)(2,1)}, u32[]{:S(2)}, u32[]{:S(2)}) collective-permute-start(bf16[8,144,256]{2,1,0:T(8,128)(2,1)} %collective-permute-done.6.refs_2_.refs_10_.refs_18_), channel_id=1, source_target_pairs={{0,1},{1,0},{2,3},{3,2},{4,5},{5,4},{6,7},{7,6},{8,9},{9,8},{10,11... | collective-permute-start | bytes 1769480 | tf_op jit(solution)/shard_map/ppermute | solution.py:39
  68.1 2.3 %collective-permute-start.13 = (bf16[1024,512]{1,0:T(8,128)(2,1)}, bf16[1024,512]{1,0:T(8,128)(2,1)}, u32[]{:S(2)}, u32[]{:S(2)}) collective-permute-start(bf16[1024,512]{1,0:T(8,128)(2,1)} %collective-permute-done.5.refs_17_), channel_id=1, source_target_pairs={{0,224},{8,232},{16,240},{24,248},{32,0},{40,8},{48,16},{56,24},{6... | collective-permute-start | bytes 3145736 | tf_op jit(solution)/shard_map/ppermute | solution.py:24
  70.6 9.2 %serve.4.refs_18_ = f32[2,4,128,512]{3,2,1,0:T(8,128)} custom-call(s32[3]{0:T(128)S(1)} %pad_add_fusion.3.at_ref, bf16[8,144,256]{2,1,0:T(8,128)(2,1)S(1)} %get-tuple-element.48.refs_0_.refs_8_.refs_16_, bf16[8,144,256]{2,1,0:T(8,128)(2,1)S(1)} %collective-permute-done.2.refs_1_.refs_9_.refs_17_, ...), custom_call_target="tpu_custom_call" | custom-call | flops 3221225472 | bytes 6291456 | tf_op jit(solution)/shard_map/serve/pallas_call | solution.py:214
  79.8 7.4 %serve.5.refs_18_ = f32[2,4,128,512]{3,2,1,0:T(8,128)} custom-call(s32[2]{0:T(128)S(1)} %pad_add_fusion.2.at_ref, bf16[8,144,256]{2,1,0:T(8,128)(2,1)S(1)} %get-tuple-element.48.refs_0_.refs_8_.refs_16_, bf16[8,144,256]{2,1,0:T(8,128)(2,1)S(1)} %collective-permute-done.2.refs_1_.refs_9_.refs_17_, ...), custom_call_target="tpu_custom_call" | custom-call | flops 2147483648 | bytes 4194304 | tf_op jit(solution)/shard_map/serve/pallas_call | solution.py:214
  87.2 6.9 %collective-permute-done.12.first_ref.refs_16_ = bf16[1024,512]{1,0:T(8,128)(2,1)} collective-permute-done((bf16[1024,512]{1,0:T(8,128)(2,1)}, bf16[1024,512]{1,0:T(8,128)(2,1)}, u32[]{:S(2)}, u32[]{:S(2)}) %collective-permute-start.12) | collective-permute-done | bytes 1048608 | tf_op jit(solution)/shard_map/ppermute | solution.py:24
  94.1 3.4 %split.1 = (bf16[512,512]{1,0:T(8,128)(2,1)}, bf16[512,512]{1,0:T(8,128)(2,1)}) custom-call(bf16[1024,512]{1,0:T(8,128)(2,1)} %collective-permute-done.12.first_ref.refs_16_, bf16[1024,512]{1,0:T(8,128)(2,1)} %collective-permute-done.13.second_ref.refs_17_), custom_call_target="tpu_custom_call" | custom-call | bytes 2097152 | tf_op jit(solution)/shard_map/split/pallas_call | solution.py:120
  97.5 1.9 %collective-permute-start.14 = (bf16[512,512]{1,0:T(8,128)(2,1)}, bf16[512,512]{1,0:T(8,128)(2,1)}, u32[]{:S(2)}, u32[]{:S(2)}) collective-permute-start(bf16[512,512]{1,0:T(8,128)(2,1)} %get-tuple-element.56), channel_id=1, source_target_pairs={{0,32},{8,40},{16,48},{24,56},{32,64},{40,72},{48,80},{56,88},{64,... | collective-permute-start | bytes 1572872 | tf_op jit(solution)/shard_map/ppermute | solution.py:24
  100.3 7.5 %serve.6.refs_10_ = f32[2,4,128,512]{3,2,1,0:T(8,128)} custom-call(s32[2]{0:T(128)S(1)} %pad_add_fusion.4.at_ref, bf16[8,144,256]{2,1,0:T(8,128)(2,1)S(1)} %get-tuple-element.48.refs_0_.refs_8_.refs_16_, bf16[8,144,256]{2,1,0:T(8,128)(2,1)S(1)} %collective-permute-done.2.refs_1_.refs_9_.refs_17_, ...), custom_call_target="tpu_custom_call" | custom-call | flops 2147483648 | bytes 4194304 | tf_op jit(solution)/shard_map/serve/pallas_call | solution.py:214
  107.7 4.0 %collective-permute-done.14.refs_8_ = bf16[512,512]{1,0:T(8,128)(2,1)} collective-permute-done((bf16[512,512]{1,0:T(8,128)(2,1)}, bf16[512,512]{1,0:T(8,128)(2,1)}, u32[]{:S(2)}, u32[]{:S(2)}) %collective-permute-start.14) | collective-permute-done | bytes 524320 | tf_op jit(solution)/shard_map/ppermute | solution.py:24
  112.1 3.9 %serve.7 = (f32[2,128,512]{2,1,0:T(8,128)S(1)}, bf16[2,128,512]{2,1,0:T(8,128)(2,1)S(1)}, bf16[2,128,512]{2,1,0:T(8,128)(2,1)S(1)}, bf16[2,128,512]{2,1,0:T(8,128)(2,1)S(1)}) custom-call(s32[1]{0:T(128)} %bitcast.10.at_ref, bf16[8,144,256]{2,1,0:T(8,128)(2,1)S(1)} %get-tuple-element.48.refs_0_.refs_8_.refs_16_, ...), custom_call_target="tpu_custom_call" | custom-call | flops 1073741824 | bytes 2097152 | tf_op jit(solution)/shard_map/serve/pallas_call | solution.py:214
  116.0 2.7 %collective-permute-start.16 = (bf16[2,128,512]{2,1,0:T(8,128)(2,1)S(1)}, bf16[2,128,512]{2,1,0:T(8,128)(2,1)S(1)}, u32[]{:S(2)}, u32[]{:S(2)}) collective-permute-start(bf16[2,128,512]{2,1,0:T(8,128)(2,1)S(1)} %get-tuple-element.60), channel_id=1, source_target_pairs={{0,24},{8,0},{16,8},{24,16},{32,56},{40,32},{48,40},{56,48},{64,88... | collective-permute-start | bytes 786440 | tf_op jit(solution)/shard_map/ppermute | solution.py:29
  119.5 4.1 %collective-permute-done.16.refs_0_ = bf16[2,128,512]{2,1,0:T(8,128)(2,1)S(1)} collective-permute-done((bf16[2,128,512]{2,1,0:T(8,128)(2,1)S(1)}, bf16[2,128,512]{2,1,0:T(8,128)(2,1)S(1)}, u32[]{:S(2)}, u32[]{:S(2)}) %collective-permute-start.16) | collective-permute-done | bytes 262176 | tf_op jit(solution)/shard_map/ppermute | solution.py:29
  123.6 2.2 %collective-permute-done.17.refs_1_ = bf16[2,128,512]{2,1,0:T(8,128)(2,1)S(1)} collective-permute-done((bf16[2,128,512]{2,1,0:T(8,128)(2,1)S(1)}, bf16[2,128,512]{2,1,0:T(8,128)(2,1)S(1)}, u32[]{:S(2)}, u32[]{:S(2)}) %collective-permute-start.17) | collective-permute-done | bytes 262176 | tf_op jit(solution)/shard_map/ppermute | solution.py:29
  125.8 8.2 %collective-permute-done.18.refs_2_ = bf16[2,128,512]{2,1,0:T(8,128)(2,1)S(1)} collective-permute-done((bf16[2,128,512]{2,1,0:T(8,128)(2,1)S(1)}, bf16[2,128,512]{2,1,0:T(8,128)(2,1)S(1)}, u32[]{:S(2)}, u32[]{:S(2)}) %collective-permute-start.18) | collective-permute-done | bytes 262176 | tf_op jit(solution)/shard_map/ppermute | solution.py:29
  135.8 2.8 %collective-permute-start.24 = (bf16[2,128,512]{2,1,0:T(8,128)(2,1)S(1)}, bf16[2,128,512]{2,1,0:T(8,128)(2,1)S(1)}, u32[]{:S(2)}, u32[]{:S(2)}) collective-permute-start(bf16[2,128,512]{2,1,0:T(8,128)(2,1)S(1)} %mix.1.mine_ref.refs_0_), channel_id=1, source_target_pairs={{0,4},{1,5},{2,6},{3,7},{4,0},{5,1},{6,2},{7,3},{8,12},{9,13},{10,... | collective-permute-start | bytes 786440 | tf_op jit(solution)/shard_map/ppermute | solution.py:34
  138.9 2.4 %collective-permute-start.22 = (bf16[2,128,512]{2,1,0:T(8,128)(2,1)S(1)}, bf16[2,128,512]{2,1,0:T(8,128)(2,1)}, u32[]{:S(2)}, u32[]{:S(2)}) collective-permute-start(bf16[2,128,512]{2,1,0:T(8,128)(2,1)S(1)} %mix.1.mine_ref.refs_0_), channel_id=1, source_target_pairs={{0,6},{1,7},{2,0},{3,1},{4,2},{5,3},{6,4},{7,5},{8,14},{9,15},{10,... | collective-permute-start | bytes 786440 | tf_op jit(solution)/shard_map/ppermute | solution.py:34
  142.9 2.8 %back.1 = bf16[128,1024]{1,0:T(8,128)(2,1)} custom-call(s32[18]{0:T(128)S(1)} %pad_add_fusion.1.at_ref, bf16[1024,1024]{1,0:T(8,128)(2,1)S(1)} %copy-done.1, bf16[2,128,512]{2,1,0:T(8,128)(2,1)S(1)} %mix.1.mine_ref.refs_0_, bf16[2,128,512]{2,1,0:T(8,128)(2,1)S(1)} %collective-permute-done.19.other_ref.refs_1_, bf16[128,1024]{1,0:T(8,128)(2,1)S(1)} %copy-done.2, ...), custom_call_target="tpu_custom_call" | custom-call | flops 805306368 | bytes 4194304 | tf_op jit(solution)/shard_map/back/pallas_call | solution.py:356
  146.6 4.7 %collective-permute-done.20.refs_2_ = bf16[2,128,512]{2,1,0:T(8,128)(2,1)} collective-permute-done((bf16[2,128,512]{2,1,0:T(8,128)(2,1)S(1)}, bf16[2,128,512]{2,1,0:T(8,128)(2,1)}, u32[]{:S(2)}, u32[]{:S(2)}) %collective-permute-start.20) | collective-permute-done | bytes 262176 | tf_op jit(solution)/shard_map/ppermute | solution.py:34
  153.6 2.9 %term.1 = (f32[256,128]{1,0:T(8,128)S(1)}, f32[256,128]{1,0:T(8,128)S(1)}, f32[256,128]{1,0:T(8,128)S(1)}, f32[256,128]{1,0:T(8,128)S(1)}) custom-call(s32[18]{0:T(128)S(1)} %pad_add_fusion.1.at_ref, bf16[1024,128]{1,0:T(8,128)(2,1)S(1)} %copy-done.3, bf16[8,128,128]{2,1,0:T(8,128)(2,1)} %bitcast.9.grads_ref, bf16[2,128,512]{2,1,0:T(8,128)(2,1)S(1)} %mix.1.mine_ref.refs_0_, ...), custom_call_target="tpu_custom_call" | custom-call | flops 536870912 | bytes 3145728 | tf_op jit(solution)/shard_map/term/pallas_call | solution.py:298
  158.0 5.6 %fresh.1 = bf16[8,128,1024]{2,1,0:T(8,128)(2,1)} custom-call(s32[18]{0:T(128)S(1)} %pad_add_fusion.1.at_ref, bf16[1024,1024]{1,0:T(8,128)(2,1)} %all-gather.2.cloned.1.call-done.weight_ref, bf16[2,128,512]{2,1,0:T(8,128)(2,1)S(1)} %mix.1.mine_ref.refs_0_, bf16[2,128,512]{2,1,0:T(8,128)(2,1)S(1)} %collective-permute-done.19.other_ref.refs_1_, ...), custom_call_target="tpu_custom_call" | custom-call | flops 2147483648 | bytes 6291456 | tf_op jit(solution)/shard_map/fresh/pallas_call | solution.py:326
  163.6 3.0 %collective-permute-done.28 = f32[256,128]{1,0:T(8,128)S(1)} collective-permute-done((f32[256,128]{1,0:T(8,128)S(1)}, f32[256,128]{1,0:T(8,128)S(1)}, u32[]{:S(2)}, u32[]{:S(2)}) %collective-permute-start.28) | collective-permute-done | bytes 131104 | tf_op jit(solution)/shard_map/ppermute | solution.py:29
  166.6 12.2 %all_to_all.25 = f32[8,32,128]{2,1,0:T(8,128)S(1)} all-to-all(f32[8,32,128]{2,1,0:T(8,128)S(1)} %bitcast.28), channel_id=1, replica_groups={{0,32,64,96,128,160,192,224},{8,40,72,104,136,168,200,232},{16,48,80,11..., dimensions={0} | all-to-all | bytes 262144 | tf_op jit(solution)/shard_map/all_to_all | solution.py:444
  (99 shorter events, 27.7 us)
Async XLA Ops:
  7.2 134.1 %all-gather.2.cloned.1.call-start = ((), (), s32[]{:S(2)}) async-start(), calls=%async_computation.2 | async-start | bytes 2359296 | tf_op jit(solution)/shard_map/all_gather | solution.py:402
  9.8 30.7 %collective-permute-start = (bf16[1024,512]{1,0:T(8,128)(2,1)}, bf16[1024,512]{1,0:T(8,128)(2,1)}, u32[]{:S(2)}, u32[]{:S(2)}) collective-permute-start(bf16[1024,512]{1,0:T(8,128)(2,1)} %bitcast.5.refs_24_), channel_id=1, source_target_pairs={{0,32},{8,40},{16,48},{24,56},{32,64},{40,72},{48,80},{56,88},{64,... | collective-permute-start | bytes 3145736 | tf_op jit(solution)/shard_map/ppermute | solution.py:24
  12.3 28.3 %collective-permute-start.1 = (bf16[1024,512]{1,0:T(8,128)(2,1)}, bf16[1024,512]{1,0:T(8,128)(2,1)}, u32[]{:S(2)}, u32[]{:S(2)}) collective-permute-start(bf16[1024,512]{1,0:T(8,128)(2,1)} %bitcast.5.refs_24_), channel_id=1, source_target_pairs={{0,224},{8,232},{16,240},{24,248},{32,0},{40,8},{48,16},{56,24},{6... | collective-permute-start | bytes 3145736 | tf_op jit(solution)/shard_map/ppermute | solution.py:24
  17.6 31.1 %copy-start.2 = (bf16[128,1024]{1,0:T(8,128)(2,1)S(1)}, bf16[128,1024]{1,0:T(8,128)(2,1)}, u32[]{:S(2)}) copy-start(bf16[128,1024]{1,0:T(8,128)(2,1)} %grad_ref.1) | copy-start | bytes 786436
  25.1 15.4 %collective-permute-start.2 = (bf16[8,144,256]{2,1,0:T(8,128)(2,1)}, bf16[8,144,256]{2,1,0:T(8,128)(2,1)S(1)}, u32[]{:S(2)}, u32[]{:S(2)}) collective-permute-start(bf16[8,144,256]{2,1,0:T(8,128)(2,1)} %get-tuple-element.39), channel_id=1, source_target_pairs={{0,8},{8,16},{16,24},{24,0},{32,40},{40,48},{48,56},{56,32},{64,72... | collective-permute-start | bytes 1769480 | tf_op jit(solution)/shard_map/ppermute | solution.py:29
  26.4 14.1 %collective-permute-start.3 = (bf16[8,144,256]{2,1,0:T(8,128)(2,1)}, bf16[8,144,256]{2,1,0:T(8,128)(2,1)}, u32[]{:S(2)}, u32[]{:S(2)}) collective-permute-start(bf16[8,144,256]{2,1,0:T(8,128)(2,1)} %get-tuple-element.40), channel_id=1, source_target_pairs={{0,24},{8,0},{16,8},{24,16},{32,56},{40,32},{48,40},{56,48},{64,88... | collective-permute-start | bytes 1769480 | tf_op jit(solution)/shard_map/ppermute | solution.py:29
  40.6 24.4 %collective-permute-start.4 = (bf16[1024,512]{1,0:T(8,128)(2,1)}, bf16[1024,512]{1,0:T(8,128)(2,1)}, u32[]{:S(2)}, u32[]{:S(2)}) collective-permute-start(bf16[1024,512]{1,0:T(8,128)(2,1)} %collective-permute-done.refs_25_), channel_id=1, source_target_pairs={{0,32},{8,40},{16,48},{24,56},{32,64},{40,72},{48,80},{56,88},{64,... | collective-permute-start | bytes 3145736 | tf_op jit(solution)/shard_map/ppermute | solution.py:24
  40.7 24.3 %collective-permute-start.5 = (bf16[1024,512]{1,0:T(8,128)(2,1)}, bf16[1024,512]{1,0:T(8,128)(2,1)}, u32[]{:S(2)}, u32[]{:S(2)}) collective-permute-start(bf16[1024,512]{1,0:T(8,128)(2,1)} %collective-permute-done.1.refs_26_), channel_id=1, source_target_pairs={{0,224},{8,232},{16,240},{24,248},{32,0},{40,8},{48,16},{56,24},{6... | collective-permute-start | bytes 3145736 | tf_op jit(solution)/shard_map/ppermute | solution.py:24
  43.3 14.2 %collective-permute-start.6 = (bf16[8,144,256]{2,1,0:T(8,128)(2,1)}, bf16[8,144,256]{2,1,0:T(8,128)(2,1)}, u32[]{:S(2)}, u32[]{:S(2)}) collective-permute-start(bf16[8,144,256]{2,1,0:T(8,128)(2,1)} %copy-done.11), channel_id=1, source_target_pairs={{0,16},{8,24},{16,0},{24,8},{32,48},{40,56},{48,32},{56,40},{64,80... | collective-permute-start | bytes 1769480 | tf_op jit(solution)/shard_map/ppermute | solution.py:29
  45.6 22.5 %collective-permute-start.8 = (bf16[8,144,256]{2,1,0:T(8,128)(2,1)S(1)}, bf16[8,144,256]{2,1,0:T(8,128)(2,1)}, u32[]{:S(2)}, u32[]{:S(2)}) collective-permute-start(bf16[8,144,256]{2,1,0:T(8,128)(2,1)S(1)} %get-tuple-element.48.refs_0_.refs_8_.refs_16_), channel_id=1, source_target_pairs={{0,1},{1,0},{2,3},{3,2},{4,5},{5,4},{6,7},{7,6},{8,9},{9,8},{10,11... | collective-permute-start | bytes 1769480 | tf_op jit(solution)/shard_map/ppermute | solution.py:39
  48.6 7.4 %collective-permute-start.7 = (f32[128,640]{1,0:T(8,128)}, f32[128,640]{1,0:T(8,128)}, u32[]{:S(2)}, u32[]{:S(2)}) collective-permute-start(f32[128,640]{1,0:T(8,128)} %copy-done.12), channel_id=1, source_target_pairs={{0,1},{1,0},{2,3},{3,2},{4,5},{5,4},{6,7},{7,6},{8,9},{9,8},{10,11... | collective-permute-start | bytes 983048 | tf_op jit(solution)/shard_map/ppermute | solution.py:39
  51.3 11.4 %all-to-all-start = ((bf16[128,8,128]{2,0,1:T(8,128)(2,1)}), bf16[128,8,128]{2,0,1:T(8,128)(2,1)}, u32[]{:S(2)}, u32[]{:S(2)}) async-start(bf16[128,8,128]{2,0,1:T(8,128)(2,1)} %copy.15), calls=%async_computation | async-start | bytes 524288 | tf_op jit(solution)/shard_map/all_to_all | solution.py:403
  56.1 14.5 %collective-permute-start.11 = (bf16[8,144,256]{2,1,0:T(8,128)(2,1)}, bf16[8,144,256]{2,1,0:T(8,128)(2,1)}, u32[]{:S(2)}, u32[]{:S(2)}) collective-permute-start(bf16[8,144,256]{2,1,0:T(8,128)(2,1)} %collective-permute-done.3.refs_3_.refs_11_.refs_19_), channel_id=1, source_target_pairs={{0,1},{1,0},{2,3},{3,2},{4,5},{5,4},{6,7},{7,6},{8,9},{9,8},{10,11... | collective-permute-start | bytes 1769480 | tf_op jit(solution)/shard_map/ppermute | solution.py:39
  57.6 13.0 %collective-permute-start.9 = (bf16[8,144,256]{2,1,0:T(8,128)(2,1)S(1)}, bf16[8,144,256]{2,1,0:T(8,128)(2,1)}, u32[]{:S(2)}, u32[]{:S(2)}) collective-permute-start(bf16[8,144,256]{2,1,0:T(8,128)(2,1)S(1)} %collective-permute-done.2.refs_1_.refs_9_.refs_17_), channel_id=1, source_target_pairs={{0,1},{1,0},{2,3},{3,2},{4,5},{5,4},{6,7},{7,6},{8,9},{9,8},{10,11... | collective-permute-start | bytes 1769480 | tf_op jit(solution)/shard_map/ppermute | solution.py:39
  65.0 5.6 %collective-permute-start.10 = (bf16[8,144,256]{2,1,0:T(8,128)(2,1)}, bf16[8,144,256]{2,1,0:T(8,128)(2,1)}, u32[]{:S(2)}, u32[]{:S(2)}) collective-permute-start(bf16[8,144,256]{2,1,0:T(8,128)(2,1)} %collective-permute-done.6.refs_2_.refs_10_.refs_18_), channel_id=1, source_target_pairs={{0,1},{1,0},{2,3},{3,2},{4,5},{5,4},{6,7},{7,6},{8,9},{9,8},{10,11... | collective-permute-start | bytes 1769480 | tf_op jit(solution)/shard_map/ppermute | solution.py:39
  67.8 26.3 %collective-permute-start.12 = (bf16[1024,512]{1,0:T(8,128)(2,1)}, bf16[1024,512]{1,0:T(8,128)(2,1)}, u32[]{:S(2)}, u32[]{:S(2)}) collective-permute-start(bf16[1024,512]{1,0:T(8,128)(2,1)} %collective-permute-done.4.refs_16_), channel_id=1, source_target_pairs={{0,32},{8,40},{16,48},{24,56},{32,64},{40,72},{48,80},{56,88},{64,... | collective-permute-start | bytes 3145736 | tf_op jit(solution)/shard_map/ppermute | solution.py:24
  68.1 26.0 %collective-permute-start.13 = (bf16[1024,512]{1,0:T(8,128)(2,1)}, bf16[1024,512]{1,0:T(8,128)(2,1)}, u32[]{:S(2)}, u32[]{:S(2)}) collective-permute-start(bf16[1024,512]{1,0:T(8,128)(2,1)} %collective-permute-done.5.refs_17_), channel_id=1, source_target_pairs={{0,224},{8,232},{16,240},{24,248},{32,0},{40,8},{48,16},{56,24},{6... | collective-permute-start | bytes 3145736 | tf_op jit(solution)/shard_map/ppermute | solution.py:24
  97.5 14.2 %collective-permute-start.14 = (bf16[512,512]{1,0:T(8,128)(2,1)}, bf16[512,512]{1,0:T(8,128)(2,1)}, u32[]{:S(2)}, u32[]{:S(2)}) collective-permute-start(bf16[512,512]{1,0:T(8,128)(2,1)} %get-tuple-element.56), channel_id=1, source_target_pairs={{0,32},{8,40},{16,48},{24,56},{32,64},{40,72},{48,80},{56,88},{64,... | collective-permute-start | bytes 1572872 | tf_op jit(solution)/shard_map/ppermute | solution.py:24
  99.4 12.7 %collective-permute-start.15 = (bf16[512,512]{1,0:T(8,128)(2,1)}, bf16[512,512]{1,0:T(8,128)(2,1)}, u32[]{:S(2)}, u32[]{:S(2)}) collective-permute-start(bf16[512,512]{1,0:T(8,128)(2,1)} %get-tuple-element.57), channel_id=1, source_target_pairs={{0,224},{8,232},{16,240},{24,248},{32,0},{40,8},{48,16},{56,24},{6... | collective-permute-start | bytes 1572872 | tf_op jit(solution)/shard_map/ppermute | solution.py:24
  116.0 7.6 %collective-permute-start.16 = (bf16[2,128,512]{2,1,0:T(8,128)(2,1)S(1)}, bf16[2,128,512]{2,1,0:T(8,128)(2,1)S(1)}, u32[]{:S(2)}, u32[]{:S(2)}) collective-permute-start(bf16[2,128,512]{2,1,0:T(8,128)(2,1)S(1)} %get-tuple-element.60), channel_id=1, source_target_pairs={{0,24},{8,0},{16,8},{24,16},{32,56},{40,32},{48,40},{56,48},{64,88... | collective-permute-start | bytes 786440 | tf_op jit(solution)/shard_map/ppermute | solution.py:29
  118.7 7.1 %collective-permute-start.17 = (bf16[2,128,512]{2,1,0:T(8,128)(2,1)S(1)}, bf16[2,128,512]{2,1,0:T(8,128)(2,1)S(1)}, u32[]{:S(2)}, u32[]{:S(2)}) collective-permute-start(bf16[2,128,512]{2,1,0:T(8,128)(2,1)S(1)} %get-tuple-element.61), channel_id=1, source_target_pairs={{0,16},{8,24},{16,0},{24,8},{32,48},{40,56},{48,32},{56,40},{64,80... | collective-permute-start | bytes 786440 | tf_op jit(solution)/shard_map/ppermute | solution.py:29
  119.1 15.0 %collective-permute-start.18 = (bf16[2,128,512]{2,1,0:T(8,128)(2,1)S(1)}, bf16[2,128,512]{2,1,0:T(8,128)(2,1)S(1)}, u32[]{:S(2)}, u32[]{:S(2)}) collective-permute-start(bf16[2,128,512]{2,1,0:T(8,128)(2,1)S(1)} %get-tuple-element.62), channel_id=1, source_target_pairs={{0,8},{8,16},{16,24},{24,0},{32,40},{40,48},{48,56},{56,32},{64,72... | collective-permute-start | bytes 786440 | tf_op jit(solution)/shard_map/ppermute | solution.py:29
  135.2 6.1 %collective-permute-start.19 = (bf16[2,128,512]{2,1,0:T(8,128)(2,1)S(1)}, bf16[2,128,512]{2,1,0:T(8,128)(2,1)S(1)}, u32[]{:S(2)}, u32[]{:S(2)}) collective-permute-start(bf16[2,128,512]{2,1,0:T(8,128)(2,1)S(1)} %mix.1.mine_ref.refs_0_), channel_id=1, source_target_pairs={{0,1},{1,0},{2,3},{3,2},{4,5},{5,4},{6,7},{7,6},{8,9},{9,8},{10,11... | collective-permute-start | bytes 786440 | tf_op jit(solution)/shard_map/ppermute | solution.py:39
  135.8 9.8 %collective-permute-start.24 = (bf16[2,128,512]{2,1,0:T(8,128)(2,1)S(1)}, bf16[2,128,512]{2,1,0:T(8,128)(2,1)S(1)}, u32[]{:S(2)}, u32[]{:S(2)}) collective-permute-start(bf16[2,128,512]{2,1,0:T(8,128)(2,1)S(1)} %mix.1.mine_ref.refs_0_), channel_id=1, source_target_pairs={{0,4},{1,5},{2,6},{3,7},{4,0},{5,1},{6,2},{7,3},{8,12},{9,13},{10,... | collective-permute-start | bytes 786440 | tf_op jit(solution)/shard_map/ppermute | solution.py:34
  138.6 12.7 %collective-permute-start.20 = (bf16[2,128,512]{2,1,0:T(8,128)(2,1)S(1)}, bf16[2,128,512]{2,1,0:T(8,128)(2,1)}, u32[]{:S(2)}, u32[]{:S(2)}) collective-permute-start(bf16[2,128,512]{2,1,0:T(8,128)(2,1)S(1)} %mix.1.mine_ref.refs_0_), channel_id=1, source_target_pairs={{0,2},{1,3},{2,4},{3,5},{4,6},{5,7},{6,0},{7,1},{8,10},{9,11},{10,... | collective-permute-start | bytes 786440 | tf_op jit(solution)/shard_map/ppermute | solution.py:34
  138.9 12.9 %collective-permute-start.22 = (bf16[2,128,512]{2,1,0:T(8,128)(2,1)S(1)}, bf16[2,128,512]{2,1,0:T(8,128)(2,1)}, u32[]{:S(2)}, u32[]{:S(2)}) collective-permute-start(bf16[2,128,512]{2,1,0:T(8,128)(2,1)S(1)} %mix.1.mine_ref.refs_0_), channel_id=1, source_target_pairs={{0,6},{1,7},{2,0},{3,1},{4,2},{5,3},{6,4},{7,5},{8,14},{9,15},{10,... | collective-permute-start | bytes 786440 | tf_op jit(solution)/shard_map/ppermute | solution.py:34
  145.7 6.3 %collective-permute-start.25 = (bf16[2,128,512]{2,1,0:T(8,128)(2,1)S(1)}, bf16[2,128,512]{2,1,0:T(8,128)(2,1)S(1)}, u32[]{:S(2)}, u32[]{:S(2)}) collective-permute-start(bf16[2,128,512]{2,1,0:T(8,128)(2,1)S(1)} %collective-permute-done.24.refs_6_), channel_id=1, source_target_pairs={{0,1},{1,0},{2,3},{3,2},{4,5},{5,4},{6,7},{7,6},{8,9},{9,8},{10,11... | collective-permute-start | bytes 786440 | tf_op jit(solution)/shard_map/ppermute | solution.py:39
  151.3 1.8 collective-permute-start.21
  151.8 1.7 collective-permute-start.23
  156.4 7.1 %collective-permute-start.26 = (f32[256,128]{1,0:T(8,128)S(1)}, f32[256,128]{1,0:T(8,128)S(1)}, u32[]{:S(2)}, u32[]{:S(2)}) collective-permute-start(f32[256,128]{1,0:T(8,128)S(1)} %get-tuple-element.66), channel_id=1, source_target_pairs={{0,24},{8,0},{16,8},{24,16},{32,56},{40,32},{48,40},{56,48},{64,88... | collective-permute-start | bytes 393224 | tf_op jit(solution)/shard_map/ppermute | solution.py:29
  156.8 6.7 %collective-permute-start.27 = (f32[256,128]{1,0:T(8,128)S(1)}, f32[256,128]{1,0:T(8,128)S(1)}, u32[]{:S(2)}, u32[]{:S(2)}) collective-permute-start(f32[256,128]{1,0:T(8,128)S(1)} %get-tuple-element.67), channel_id=1, source_target_pairs={{0,16},{8,24},{16,0},{24,8},{32,48},{40,56},{48,32},{56,40},{64,80... | collective-permute-start | bytes 393224 | tf_op jit(solution)/shard_map/ppermute | solution.py:29
  157.2 9.4 %collective-permute-start.28 = (f32[256,128]{1,0:T(8,128)S(1)}, f32[256,128]{1,0:T(8,128)S(1)}, u32[]{:S(2)}, u32[]{:S(2)}) collective-permute-start(f32[256,128]{1,0:T(8,128)S(1)} %get-tuple-element.68), channel_id=1, source_target_pairs={{0,8},{8,16},{16,24},{24,0},{32,40},{40,48},{48,56},{56,32},{64,72... | collective-permute-start | bytes 393224 | tf_op jit(solution)/shard_map/ppermute | solution.py:29
  (16 other events, 146.5 us)
Sparse Core Ops, SparseCore 0:
  28.0 30.4 all-gather.1
